TPU v7x, 512 devices: a whole 4x8x8 slice. The times are simulated.
512 devices in a mesh: section: 4 (over x), dp: 8 (over z_hi, core), expert: 16 (over z_lo, y).
Axes of the slice: x: 4, y: 8, z: 8 (z_hi: 4, z_lo: 2; z = z_hi * 2 + z_lo), core: 2. Of those that a mesh axis runs over, the one named last changes fastest.
Arguments:
- stream: bfloat16 [65536, 5120], P(('section', 'dp', 'expert')), may hold values from -80 to 80
- expert_rows: bfloat16 [512, 16, 12, 5120], P(('section', 'dp', 'expert')), may hold values from -6 to 6
- expert_ids: int32 [65536], P(('section', 'dp', 'expert')), may hold values from 0 to 127, as said below
- route_weight: float32 [65536], P(('section', 'dp', 'expert')), may hold values from 0.3 to 1
- norm_gain: float32 [4, 5120], P('section'), may hold values from 0.1 to 1.9
- kv_weight: bfloat16 [4, 5120, 2048], P('section', 'expert', 'dp'), may hold values from -0.078125 to 0.078125
Outputs:
- keys_values: bfloat16 [32, 16, 128, 2048], P('section', 'expert', None, 'dp')
Inputs may be any that keep to these rules, and one draw needn't show every extreme that they name: `expert_ids`: in each aligned block of 128 tokens (the tokens of one device), at most 12 tokens name experts h * 8 to (h + 1) * 8 - 1 for any h, and for some h exactly 12 do.
All inputs are finite; a program needn't handle non-finite values.
Results may differ from a plain program's by a relative error of at most 0.0057.
Values may be sent and summed in bfloat16 or wider, within the bound.
A program may use at most 64 MiB of HBM per device.

v0:
```python
import jax
import jax.numpy as jnp
from jax import lax
from jax.sharding import PartitionSpec as P

EXPERTS = 128


def shifted(value, axis, steps):
    count = lax.axis_size(axis)
    pairs = [(source, (source + steps) % count) for source in range(count)]
    return lax.ppermute(value, axis, pairs)


def slot_index(expert_ids, per_device):
    holders = expert_ids // per_device
    places = jnp.arange(expert_ids.shape[0], dtype=jnp.int32)
    earlier = (expert_ids[None, :] < expert_ids[:, None]) | (
        expert_ids[None, :] == expert_ids[:, None]
    ) & (places[None, :] < places[:, None])
    same_holder = holders[None, :] == holders[:, None]
    slots = jnp.sum((earlier & same_holder).astype(jnp.int32), axis=1)
    return (holders, slots)


def body(stream, expert_rows, expert_ids, route_weight, norm_gain, kv_weight):
    per_device = EXPERTS // lax.axis_size("expert")
    holders, slots = slot_index(expert_ids, per_device)
    returned = lax.all_to_all(expert_rows, "expert", split_axis=1, concat_axis=0, tiled=True)
    capacity = returned.shape[2]
    flat_rows = returned.reshape(-1, returned.shape[3])
    picked = jnp.take(flat_rows, holders * capacity + slots, axis=0)
    combined = (
        stream.astype(jnp.float32) + route_weight[:, None] * picked.astype(jnp.float32)
    ).astype(jnp.bfloat16)
    arrived = shifted(combined, "section", 1)
    values = arrived.astype(jnp.float32)
    scale = lax.rsqrt(jnp.mean(values * values, axis=-1, keepdims=True) + 1e-05)
    normed = (values * scale * norm_gain[0][None, :]).astype(jnp.bfloat16)
    weights_local = kv_weight[0]
    token_count = normed.shape[0]
    whole_weight = lax.all_gather(weights_local, "expert", axis=0, tiled=True)
    result = jnp.dot(
        lax.all_gather(normed, "dp", axis=0, tiled=True),
        whole_weight,
        preferred_element_type=jnp.float32,
    ).astype(jnp.bfloat16)
    return result.reshape(-1, 1, token_count, result.shape[1])


def solution(mesh):
    in_specs = (
        P(("section", "dp", "expert"), None),
        P(("section", "dp", "expert"), None, None, None),
        P(("section", "dp", "expert")),
        P(("section", "dp", "expert")),
        P("section", None),
        P("section", "expert", "dp"),
    )
    out_specs = P("section", "expert", None, "dp")
    return jax.shard_map(body, mesh=mesh, in_specs=in_specs, out_specs=out_specs, check_vma=False)
```

profile of v0, /device:TPU:1, one launch (start us, length us, event | category | flops | bytes accessed | tf_op | source)
XLA Modules:
  0.0 259.3 jit_solution(9026425537961768503)
XLA Ops:
  6.5 4.2 %copy.13 = bf16[1,16,12,5120]{3,2,0,1:T(8,128)(2,1)} copy(bf16[1,16,12,5120]{3,1,2,0:T(8,128)(2,1)} %param.7) | data formatting | bytes 3932160 | tf_op args[1]
  10.7 0.0 copy-start.1
  10.7 9.7 %all-to-all-start = ((bf16[1,16,12,5120]{3,2,0,1:T(8,128)(2,1)}), bf16[1,16,12,5120]{3,2,0,1:T(8,128)(2,1)}, u32[]{:S(2)}, u32[]{:S(2)}) async-start(bf16[1,16,12,5120]{3,2,0,1:T(8,128)(2,1)} %copy.13), calls=%async_computation | async-start | bytes 5242880 | tf_op jit(solution)/shard_map/all_to_all | solution.py:29
  20.5 0.0 all-gather.6.cloned.1.call-start
  20.5 0.7 all-gather.6.cloned.1.call-update
  21.2 0.0 all-gather.4.cloned.1.call-start
  21.2 0.0 copy-done.1
  21.3 0.2 convert_reduce_fusion
  21.5 69.3 %all-to-all-done = bf16[1,16,12,5120]{3,2,0,1:T(8,128)(2,1)} async-done(((bf16[1,16,12,5120]{3,2,0,1:T(8,128)(2,1)}), bf16[1,16,12,5120]{3,2,0,1:T(8,128)(2,1)}, u32[]{:S(2)}, u32[]{:S(2)}) %all-to-all-start) | async-done | bytes 1966112 | tf_op jit(solution)/shard_map/all_to_all | solution.py:29
  90.8 2.7 %reshape.28 = bf16[192,5120]{1,0:T(8,128)(2,1)S(1)} reshape(bf16[1,16,12,5120]{3,2,0,1:T(8,128)(2,1)} %all-to-all-done) | data formatting | bytes 3932160 | tf_op jit(solution)/shard_map/reshape | solution.py:31
  93.5 0.0 copy-start.2
  93.5 1.3 gather_fusion
  94.8 0.0 copy-done.2
  94.8 0.0 copy-start
  94.8 1.9 add_convert_fusion
  96.7 3.3 %collective-permute-start = (bf16[128,5120]{1,0:T(8,128)(2,1)S(1)}, bf16[128,5120]{1,0:T(8,128)(2,1)S(1)}, u32[]{:S(2)}, u32[]{:S(2)}) collective-permute-start(bf16[128,5120]{1,0:T(8,128)(2,1)S(1)} %add_convert_fusion), channel_id=1, source_target_pairs={{0,128},{128,256},{256,384},{384,0},{1,129},{129,257},{257,385},{3... | collective-permute-start | bytes 3932168 | tf_op jit(solution)/shard_map/ppermute | solution.py:12
  100.0 24.8 %collective-permute-done = bf16[128,5120]{1,0:T(8,128)(2,1)S(1)} collective-permute-done((bf16[128,5120]{1,0:T(8,128)(2,1)S(1)}, bf16[128,5120]{1,0:T(8,128)(2,1)S(1)}, u32[]{:S(2)}, u32[]{:S(2)}) %collective-permute-start) | collective-permute-done | bytes 1310752 | tf_op jit(solution)/shard_map/ppermute | solution.py:12
  124.8 0.3 fusion
  125.2 0.0 copy-done
  125.2 1.5 fusion.2
  126.6 0.0 all-gather.4.cloned.1.call-update
  126.6 0.0 all-gather.6.cloned.1.call-done
  126.7 117.4 %all-gather.4.cloned.1.call-done = bf16[1024,5120]{1,0:T(8,128)(2,1)} async-done(((bf16[128,5120]{1,0:T(8,128)(2,1)}), bf16[1024,5120]{1,0:T(8,128)(2,1)}) %all-gather.4.cloned.1.call-update) | async-done | bytes 10485776 | tf_op jit(solution)/shard_map/all_gather | solution.py:44
  244.1 8.4 %fusion.5 = bf16[1024,256]{1,0:T(8,128)(2,1)} fusion(bf16[1024,5120]{1,0:T(8,128)(2,1)} %all-gather.4.cloned.1.call-done, bf16[1,5120,256]{2,1,0:T(8,128)(2,1)} %all-gather.6.cloned.1.call-done), kind=kOutput, calls=%fused_computation.9 | convolution fusion | flops 2684616704 | bytes 13631488 | tf_op jit(solution)/shard_map/dot_general | solution.py:43
  (4 shorter events, 0.0 us)
Async XLA Ops:
  10.7 10.5 %copy-start.1 = (s32[128]{0:T(128)S(1)}, s32[128]{0:T(128)}, u32[]{:S(2)}) copy-start(s32[128]{0:T(128)} %param.8) | copy-start | bytes 1540
  10.7 80.1 %all-to-all-start = ((bf16[1,16,12,5120]{3,2,0,1:T(8,128)(2,1)}), bf16[1,16,12,5120]{3,2,0,1:T(8,128)(2,1)}, u32[]{:S(2)}, u32[]{:S(2)}) async-start(bf16[1,16,12,5120]{3,2,0,1:T(8,128)(2,1)} %copy.13), calls=%async_computation | async-start | bytes 5242880 | tf_op jit(solution)/shard_map/all_to_all | solution.py:29
  20.5 106.2 %all-gather.6.cloned.1.call-start = ((), (), s32[]{:S(2)}) async-start(), calls=%async_computation.2 | async-start | bytes 2785280 | tf_op jit(solution)/shard_map/all_gather | solution.py:42
  21.2 222.9 %all-gather.4.cloned.1.call-start = ((), (), s32[]{:S(2)}) async-start(), calls=%async_computation.1 | async-start | bytes 11796480 | tf_op jit(solution)/shard_map/all_gather | solution.py:44
  93.5 1.3 copy-start.2
  94.8 30.4 %copy-start = (f32[1,5120]{1,0:T(1,128)S(1)}, f32[1,5120]{1,0:T(1,128)}, u32[]{:S(2)}) copy-start(f32[1,5120]{1,0:T(1,128)} %param.10) | copy-start | bytes 61444
  96.7 28.1 %collective-permute-start = (bf16[128,5120]{1,0:T(8,128)(2,1)S(1)}, bf16[128,5120]{1,0:T(8,128)(2,1)S(1)}, u32[]{:S(2)}, u32[]{:S(2)}) collective-permute-start(bf16[128,5120]{1,0:T(8,128)(2,1)S(1)} %add_convert_fusion), channel_id=1, source_target_pairs={{0,128},{128,256},{256,384},{384,0},{1,129},{129,257},{257,385},{3... | collective-permute-start | bytes 3932168 | tf_op jit(solution)/shard_map/ppermute | solution.py:12
Sparse Core Ops, SparseCore 0:
  23.4 96.2 all-gather.5
  126.8 117.2 all-gather.3
where the time goes:
time: 260 us; the launch traced here: 259 us
  waiting for transfers between devices  212 us (82%)
  between operations  13.5 us (5%)
  starting transfers between devices  13.1 us (5%)
  matrix products  8.38 us (3%)
  local copies, waits for them, and re-layouts  8.16 us (3%)
  other arithmetic  3.91 us (2%)
    all_gather x1, waiting for transfers between devices, body(): lax.all_gather(normed, 'dp', axis=0, tiled=True)  117 us
    all_to_all x1, waiting for transfers between devices, body(): lax.all_to_all(expert_rows, 'expert', split_axis=1, concat_axis=0, tiled=...  69.3 us
    ppermute x1, waiting for transfers between devices, shifted(): return lax.ppermute(value, axis, pairs)  24.8 us
    all_to_all x1, starting transfers between devices, body(): lax.all_to_all(expert_rows, 'expert', split_axis=1, concat_axis=0, tiled=...  9.74 us
    dot_general x1, matrix products, body(): jnp.dot(lax.all_gather(normed, 'dp', axis=0, tiled=True), whole_weight, p...  8.38 us
  transfers between devices with their start and end apart: 4, of which 3 were waited for; matrix products, arithmetic and copies ran while one was open for 3% of the time, Pallas kernels for 0%

commit v1 on v0

v1 whole, which is shorter than its diff:
```python
import jax
import jax.numpy as jnp
from jax import lax
from jax.experimental import pallas as pl
from jax.experimental.pallas import tpu as pltpu
from jax.sharding import PartitionSpec as P

MESH = pl.DeviceIdType.MESH

D = 5120
TOK = 128
CAP = 12
NX, NY, NZ = 4, 8, 8
NZH = 4
NE = 16
KROWS = 320
NCOL = 256
QUART = D // 4
PACK = D * CAP // 16
CH = 256
RY = 192
EPS = 1e-05


def kernel(
    rows_ref, stream_ref, ids_ref, route_ref, gain_ref, weight_ref, out_ref,
    packed, got, weights, gain, select, normed, result,
    shift_sems, a2a_send, a2a_recv, own_sem,
    ring1_send, ring1_recv, ring2_send, ring2_recv, pair_sems, out_send, out_recv,
):
    x = lax.axis_index("section")
    d = lax.axis_index("dp")
    e = lax.axis_index("expert")
    zh, c = d // 2, d % 2
    zl, y = e // NY, e % NY
    z = zh * 2 + zl
    sign = 1 - 2 * c

    def device(x_, y_, z_, c_):
        return (x_, (z_ // 2) * 2 + c_, (z_ % 2) * NY + y_)

    def wrap(v, n):
        return lax.rem(v + 2 * n, n)

    x_next, x_prev = wrap(x + 1, NX), wrap(x - 1, NX)

    peers = [(x, d, wrap(e + k, NE)) for k in range(1, NE)]
    peers.append((x, zh * 2 + 1 - c, e))
    peers.append(device(x, y, wrap(z + 2 * zl - 1, NZ), c))
    for other in (x_next, x_prev):
        for k in range(NZH):
            peers.append((other, k * 2 + c, e))
    barrier = pltpu.get_barrier_semaphore()
    for peer in peers:
        pl.semaphore_signal(barrier, inc=1, device_id=peer, device_id_type=MESH)
    pl.semaphore_wait(barrier, len(peers))

    sends = []

    def remote(src, dst, send_sem, recv_sem, to):
        copy = pltpu.make_async_remote_copy(
            src_ref=src, dst_ref=dst, send_sem=send_sem, recv_sem=recv_sem,
            device_id=to, device_id_type=MESH,
        )
        copy.start()
        sends.append(copy)

    def arrived(dst, recv_sem):
        pltpu.make_async_remote_copy(
            src_ref=dst, dst_ref=dst, send_sem=recv_sem, recv_sem=recv_sem,
            device_id=(x, d, e), device_id_type=MESH,
        ).wait_recv()

    home = weights.at[zh, zl, y]
    remote(weight_ref, home, shift_sems.at[0], shift_sems.at[1], (x_prev, d, e))
    remote(gain_ref, gain, shift_sems.at[2], shift_sems.at[3], (x_prev, d, e))

    r = lax.broadcasted_iota(jnp.int32, (256, 256), 0)
    k = lax.broadcasted_iota(jnp.int32, (256, 256), 1)
    wanted = (r & 3) * 64 + ((r >> 2) & 3) * 16 + (r >> 4)
    order = (k == wanted).astype(jnp.bfloat16)

    def pack(i, _):
        b, n = i // 5, i % 5
        parts = [
            rows_ref[pl.ds(b * 64, 64), pl.ds(pl.multiple_of(q * QUART + n * CH, CH), CH)]
            for q in range(4)
        ]
        moved = jnp.dot(order, jnp.concatenate(parts, axis=0), preferred_element_type=jnp.float32)
        packed[:, pl.ds(pl.multiple_of(i * CH, CH), CH)] = moved.astype(jnp.bfloat16)
        return 0

    lax.fori_loop(0, 15, pack, 0)

    half = RY // 2
    rest = (KROWS - RY) // 2

    def block(axis, origin):
        if axis == "y":
            return weights.at[zh, zl, origin, pl.ds(0, RY), :]
        return weights.at[origin // 2, origin % 2, y, pl.ds(RY, KROWS - RY), :]

    def bundle(axis, origin, h):
        if axis == "z":
            return weights.at[origin // 2, origin % 2, :, pl.ds(h * half, half), :]
        return weights.at[:, :, origin, pl.ds(RY + h * rest, rest), :]

    def place(axis, steps):
        return wrap(y + steps, NY) if axis == "y" else wrap(z + steps, NZ)

    def towards(axis, steps):
        if axis == "y":
            return device(x, wrap(y + steps, NY), z, c)
        return device(x, y, wrap(z + steps, NZ), c)

    slots1 = {}
    slots2 = {}

    def send1(axis, way, step):
        s = sign if way == 0 else -sign
        i = slots1.setdefault((axis, way, step), len(slots1))
        ref = block(axis, place(axis, -s * (step - 1)))
        remote(ref, ref, ring1_send.at[i], ring1_recv.at[i], towards(axis, s))

    def recv1(axis, way, step):
        s = sign if way == 0 else -sign
        arrived(block(axis, place(axis, -s * step)), ring1_recv.at[slots1[(axis, way, step)]])

    def send2(axis, way, step, h):
        s = sign if way == 0 else -sign
        i = slots2.setdefault((axis, way, step, h), len(slots2))
        ref = bundle(axis, place(axis, -s * (step - 1)), h)
        remote(ref, ref, ring2_send.at[i], ring2_recv.at[i], towards(axis, s))

    def recv2(axis, way, step, h):
        s = sign if way == 0 else -sign
        arrived(bundle(axis, place(axis, -s * step), h), ring2_recv.at[slots2[(axis, way, step, h)]])

    count = (4, 3)
    rings = [("y", 0), ("z", 0), ("y", 1), ("z", 1)]

    arrived(home, shift_sems.at[1])
    for axis, way in rings:
        send1(axis, way, 1)

    def row_slab(ref, i):
        return ref.at[pl.ds(pl.multiple_of(i * 16, 16), 16), :]

    own = pltpu.make_async_copy(row_slab(packed, e), row_slab(got, e), own_sem)
    own.start()
    for n in range(1, NE):
        to = wrap(e + n, NE)
        remote(row_slab(packed, to), row_slab(got, e), a2a_send.at[n], a2a_recv.at[n], (x, d, to))

    for step in range(1, 5):
        for axis, way in rings:
            if step <= count[way]:
                recv1(axis, way, step)
                if step < count[way]:
                    send1(axis, way, step + 1)
    for h in range(2):
        for axis, way in rings:
            send2(axis, way, 1, h)

    ids = ids_ref[...]
    across = jnp.broadcast_to(ids, (TOK, TOK))
    down = across.T
    row_place = lax.broadcasted_iota(jnp.int32, (TOK, TOK), 0)
    col_place = lax.broadcasted_iota(jnp.int32, (TOK, TOK), 1)
    earlier = (across < down) | ((across == down) & (col_place < row_place))
    same = (across >> 3) == (down >> 3)
    slot = jnp.sum((earlier & same).astype(jnp.int32), axis=1, keepdims=True)
    holder = down[:, 0:1] >> 3
    base = (slot >> 2) * 256 + holder * 16 + (slot & 3) * 4
    kk = lax.broadcasted_iota(jnp.int32, (TOK, 768), 1)
    for q in range(4):
        select[q] = (kk == base + q).astype(jnp.bfloat16)
    route = jnp.broadcast_to(route_ref[...], (TOK, TOK)).T[:, 0:1]

    def step2(step):
        for h in range(2):
            for axis, way in rings:
                if step <= count[way]:
                    recv2(axis, way, step, h)
                    if step < count[way]:
                        send2(axis, way, step + 1, h)

    step2(1)

    own.wait()
    for n in range(1, NE):
        arrived(row_slab(got, wrap(e - n, NE)), a2a_recv.at[n])
    arrived(gain, shift_sems.at[3])

    def combine(i, total):
        q, n = i // 5, i % 5
        picked = jnp.zeros((TOK, CH), jnp.float32)
        for b in range(3):
            picked += jnp.dot(
                select[q, :, b * 256 : (b + 1) * 256],
                got[:, pl.ds(pl.multiple_of(b * QUART + n * CH, CH), CH)],
                preferred_element_type=jnp.float32,
            )
        at = pl.ds(pl.multiple_of(i * CH, CH), CH)
        both = (stream_ref[:, at].astype(jnp.float32) + route * picked).astype(jnp.bfloat16)
        normed[c, :, at] = both
        both = both.astype(jnp.float32)
        return total + both * both

    total = lax.fori_loop(0, 20, combine, jnp.zeros((TOK, CH), jnp.float32))
    scale = lax.rsqrt(jnp.sum(total, axis=1, keepdims=True) / D + EPS)

    def norm(i, _):
        at = pl.ds(pl.multiple_of(i * CH, CH), CH)
        value = normed[c, :, at].astype(jnp.float32) * scale * gain[:, at]
        normed[c, :, at] = value.astype(jnp.bfloat16)
        return 0

    lax.fori_loop(0, 20, norm, 0)
    remote(normed.at[c], normed.at[c], pair_sems.at[0], pair_sems.at[1], (x, zh * 2 + 1 - c, e))

    for step in range(2, 5):
        step2(step)

    arrived(normed.at[1 - c], pair_sems.at[1])

    for n in range(NZH):
        to = wrap(zh + 2 + n, NZH)

        def part(q, total):
            left = normed[:, :, pl.ds(pl.multiple_of(q * QUART, QUART), QUART)].reshape(2 * TOK, QUART)
            right = weights[to, q // 2, pl.ds((q % 2) * 4, 4)].reshape(QUART, NCOL)
            return total + jnp.dot(left, right, preferred_element_type=jnp.float32)

        total = lax.fori_loop(0, 4, part, jnp.zeros((2 * TOK, NCOL), jnp.float32))
        result[n] = total.astype(jnp.bfloat16).reshape(2, TOK, NCOL)
        remote(
            result.at[n], out_ref.at[pl.ds(zh * 2, 2)], out_send.at[n], out_recv.at[n],
            (x_next, to * 2 + c, e),
        )
    for n in range(NZH):
        source = wrap(zh - 2 - n, NZH)
        arrived(out_ref.at[pl.ds(source * 2, 2)], out_recv.at[n])
    for copy in sends:
        copy.wait_send()


def body(stream, expert_rows, expert_ids, route_weight, norm_gain, kv_weight):
    rows = jnp.transpose(expert_rows[0], (1, 0, 2)).reshape(CAP * NE, D)
    vmem = pl.BlockSpec(memory_space=pltpu.VMEM)
    hbm = pl.BlockSpec(memory_space=pl.ANY)
    dma = pltpu.SemaphoreType.DMA
    out = pl.pallas_call(
        kernel,
        out_shape=jax.ShapeDtypeStruct((8, TOK, NCOL), jnp.bfloat16),
        in_specs=[vmem, vmem, vmem, vmem, hbm, hbm],
        out_specs=hbm,
        scratch_shapes=[
            pltpu.VMEM((256, PACK), jnp.bfloat16),
            pltpu.VMEM((256, PACK), jnp.bfloat16),
            pltpu.VMEM((NZH, 2, NY, KROWS, NCOL), jnp.bfloat16),
            pltpu.VMEM((1, D), jnp.float32),
            pltpu.VMEM((4, TOK, 768), jnp.bfloat16),
            pltpu.VMEM((2, TOK, D), jnp.bfloat16),
            pltpu.VMEM((NZH, 2, TOK, NCOL), jnp.bfloat16),
            dma((4,)), dma((NE,)), dma((NE,)), dma,
            dma((14,)), dma((14,)), dma((28,)), dma((28,)), dma((2,)), dma((NZH,)), dma((NZH,)),
        ],
        compiler_params=pltpu.CompilerParams(
            collective_id=0, has_side_effects=True, vmem_limit_bytes=48 * 1024 * 1024
        ),
        cost_estimate=pl.CostEstimate(
            flops=2 * 1024 * D * NCOL, bytes_accessed=8 * 1024 * 1024, transcendentals=TOK
        ),
    )(
        rows, stream, expert_ids.reshape(1, TOK), route_weight.reshape(1, TOK),
        norm_gain, kv_weight[0],
    )
    return out.reshape(8, 1, TOK, NCOL)


def solution(mesh):
    in_specs = (
        P(("section", "dp", "expert"), None),
        P(("section", "dp", "expert"), None, None, None),
        P(("section", "dp", "expert")),
        P(("section", "dp", "expert")),
        P("section", None),
        P("section", "expert", "dp"),
    )
    out_specs = P("section", "expert", None, "dp")
    return jax.shard_map(body, mesh=mesh, in_specs=in_specs, out_specs=out_specs, check_vma=False)
```

time: 260 us -> 159 us (0.61)
  waiting for transfers between devices: 212 us -> 0 us
  Pallas kernels: 0 us -> 151 us
  between operations: 13.5 us -> 0.02 us
  starting transfers between devices: 13.1 us -> 0 us
  matrix products: 8.38 us -> 0 us
  other arithmetic: 3.91 us -> 0 us
    pallas_call x0 -> x1, Pallas kernels: none -> 151 us  [body(): pl.pallas_call(kernel, out_shape=jax.ShapeDtypeStruct((8, TOK, NCOL), jnp...]
    all_gather x2 -> x0, waiting for transfers between devices: 117 us -> none  [the longest x1 117 us: body(): lax.all_gather(normed, 'dp', axis=0, tiled=True)]
    all_to_all x1 -> x0, waiting for transfers between devices: 69.3 us -> none  [body(): lax.all_to_all(expert_rows, 'expert', split_axis=1, concat_axis=0, tiled=...]
    ppermute x1 -> x0, waiting for transfers between devices: 24.8 us -> none  [shifted(): return lax.ppermute(value, axis, pairs)]
    all_to_all x1 -> x0, starting transfers between devices: 9.74 us -> none  [body(): lax.all_to_all(expert_rows, 'expert', split_axis=1, concat_axis=0, tiled=...]
    dot_general x1 -> x0, matrix products: 8.38 us -> none  [body(): jnp.dot(lax.all_gather(normed, 'dp', axis=0, tiled=True), whole_weight, p...]
    convert_element_type x2 -> x0, other arithmetic: 3.35 us -> none  [the longest x1 1.9 us: body(): combined = (stream.astype(jnp.float32) + route_weight[:, None] * picked.a...]
    ppermute x1 -> x0, starting transfers between devices: 3.27 us -> none  [shifted(): return lax.ppermute(value, axis, pairs)]
  transfers between devices with their start and end apart: 4 -> 0, of which waited for: 3 -> 0; matrix products, arithmetic and copies ran while one was open for 3% -> 0% of each run, Pallas kernels for 0% -> 0%
where the time goes in v1:
time: 159 us; the launch traced here: 158 us
  Pallas kernels  151 us (95%)
  local copies, waits for them, and re-layouts  6.61 us (4%)
    pallas_call x1, Pallas kernels, body(): pl.pallas_call(kernel, out_shape=jax.ShapeDtypeStruct((8, TOK, NCOL), jnp...  151 us
    unnamed x13, local copies, waits for them, and re-layouts  6.61 us

profile of v1, /device:TPU:1, one launch (start us, length us, event | category | flops | bytes accessed | tf_op | source)
XLA Modules:
  0.0 157.7 jit_solution(14591747475533214112)
XLA Ops:
  0.0 0.0 copy-start
  0.0 1.5 copy-done
  1.5 0.0 copy-start.1
  1.5 1.3 copy-done.1
  2.9 0.0 copy-start.2
  2.9 0.9 copy-done.2
  3.8 0.0 copy-start.3
  3.8 0.7 copy-done.3
  4.5 0.0 copy-start.4
  4.5 0.7 copy-done.4
  5.2 0.0 copy-start.5
  5.2 0.7 copy-done.5
  5.8 151.1 %shard_map.64 = bf16[8,128,256]{2,1,0:T(8,128)(2,1)S(1)} custom-call(bf16[192,5120]{1,0:T(8,128)(2,1)S(1)} %bitcast.12, bf16[128,5120]{1,0:T(8,128)(2,1)S(1)} %copy-done.1, s32[1,128]{1,0:T(1,128)S(1)} %bitcast.14, f32[1,128]{1,0:T(1,128)S(1)} %bitcast.15, f32[1,5120]{1,0:T(1,128)S(1)} %copy-done.3, bf16[320,256]{1,0:T(8,128)(2,1)S(1)} %bitcast.13), custom_call_target="tpu_custom_call" | custom-call | flops 2684354560 | bytes 8388608 | tf_op jit(solution)/shard_map/pallas_call | solution.py:253
  156.9 0.8 copy.9
Async XLA Ops:
  0.0 1.5 copy-start
  1.5 1.3 copy-start.1
  2.9 0.9 copy-start.2
  3.8 0.7 copy-start.3
  4.5 0.7 copy-start.4
  5.2 0.7 copy-start.5

commit v2 on v1

--- a/solution.py
+++ b/solution.py
@@ -18,14 +18,18 @@
 QUART = D // 4
 PACK = D * CAP // 16
 CH = 256
-RY = 192
+RY = 160
 EPS = 1e-05
+ROW_ORDER = (4, 12, 3, 13, 5, 11, 2, 14, 6, 10, 1, 15, 7, 9, 8)
+ROWS_EARLY = 2
+ROWS_STEP = 2
+COMBINE_AT = 2
 
 
 def kernel(
-    rows_ref, stream_ref, ids_ref, route_ref, gain_ref, weight_ref, out_ref,
-    packed, got, weights, gain, select, normed, result,
-    shift_sems, a2a_send, a2a_recv, own_sem,
+    rows_hbm, stream_hbm, ids_hbm, route_hbm, gain_ref, weight_ref, out_ref,
+    rows_ref, stream_ref, ids_ref, route_ref, packed, got, weights, gain, select, normed, result,
+    load_sems, shift_sems, a2a_send, a2a_recv, own_sem,
     ring1_send, ring1_recv, ring2_send, ring2_recv, pair_sems, out_send, out_recv,
 ):
     x = lax.axis_index("section")
@@ -43,6 +47,11 @@
         return lax.rem(v + 2 * n, n)
 
     x_next, x_prev = wrap(x + 1, NX), wrap(x - 1, NX)
+
+    pairs = [(ids_hbm, ids_ref), (route_hbm, route_ref), (rows_hbm, rows_ref), (stream_hbm, stream_ref)]
+    loads = [pltpu.make_async_copy(src, dst, load_sems.at[i]) for i, (src, dst) in enumerate(pairs)]
+    for load in loads:
+        load.start()
 
     peers = [(x, d, wrap(e + k, NE)) for k in range(1, NE)]
     peers.append((x, zh * 2 + 1 - c, e))
@@ -90,6 +99,7 @@
         packed[:, pl.ds(pl.multiple_of(i * CH, CH), CH)] = moved.astype(jnp.bfloat16)
         return 0
 
+    loads[2].wait()
     lax.fori_loop(0, 15, pack, 0)
 
     half = RY // 2
@@ -137,31 +147,28 @@
         arrived(bundle(axis, place(axis, -s * step), h), ring2_recv.at[slots2[(axis, way, step, h)]])
 
     count = (4, 3)
-    rings = [("y", 0), ("z", 0), ("y", 1), ("z", 1)]
+    rings = [("z", 0), ("z", 1), ("y", 0), ("y", 1)]
+
+    def row_slab(ref, i):
+        return ref.at[pl.ds(pl.multiple_of(i * 16, 16), 16), :]
+
+    own = pltpu.make_async_copy(row_slab(packed, e), row_slab(got, e), own_sem)
+    own.start()
+    left = list(range(1, NE))
+
+    def send_rows(many):
+        for n in left[:many]:
+            to = wrap(e + ROW_ORDER[n - 1], NE)
+            remote(row_slab(packed, to), row_slab(got, e), a2a_send.at[n], a2a_recv.at[n], (x, d, to))
+        del left[:many]
 
     arrived(home, shift_sems.at[1])
     for axis, way in rings:
         send1(axis, way, 1)
-
-    def row_slab(ref, i):
-        return ref.at[pl.ds(pl.multiple_of(i * 16, 16), 16), :]
-
-    own = pltpu.make_async_copy(row_slab(packed, e), row_slab(got, e), own_sem)
-    own.start()
-    for n in range(1, NE):
-        to = wrap(e + n, NE)
-        remote(row_slab(packed, to), row_slab(got, e), a2a_send.at[n], a2a_recv.at[n], (x, d, to))
-
-    for step in range(1, 5):
-        for axis, way in rings:
-            if step <= count[way]:
-                recv1(axis, way, step)
-                if step < count[way]:
-                    send1(axis, way, step + 1)
-    for h in range(2):
-        for axis, way in rings:
-            send2(axis, way, 1, h)
-
+    send_rows(ROWS_EARLY)
+
+    loads[0].wait()
+    loads[1].wait()
     ids = ids_ref[...]
     across = jnp.broadcast_to(ids, (TOK, TOK))
     down = across.T
@@ -177,20 +184,35 @@
         select[q] = (kk == base + q).astype(jnp.bfloat16)
     route = jnp.broadcast_to(route_ref[...], (TOK, TOK)).T[:, 0:1]
 
-    def step2(step):
+    for step in range(1, 5):
+        for axis, way in rings:
+            if step <= count[way]:
+                recv1(axis, way, step)
+                if step < count[way]:
+                    send1(axis, way, step + 1)
+        if step < 4:
+            send_rows(ROWS_STEP)
+    for h in range(2):
+        for axis, way in rings:
+            send2(axis, way, 1, h)
+    send_rows(NE)
+
+    def step2(step, axes="zy"):
         for h in range(2):
             for axis, way in rings:
-                if step <= count[way]:
+                if step <= count[way] and axis in axes:
                     recv2(axis, way, step, h)
                     if step < count[way]:
                         send2(axis, way, step + 1, h)
 
-    step2(1)
+    for step in range(1, COMBINE_AT + 1):
+        step2(step)
 
     own.wait()
     for n in range(1, NE):
-        arrived(row_slab(got, wrap(e - n, NE)), a2a_recv.at[n])
+        arrived(row_slab(got, wrap(e - ROW_ORDER[n - 1], NE)), a2a_recv.at[n])
     arrived(gain, shift_sems.at[3])
+    loads[3].wait()
 
     def combine(i, total):
         q, n = i // 5, i % 5
@@ -219,13 +241,11 @@
     lax.fori_loop(0, 20, norm, 0)
     remote(normed.at[c], normed.at[c], pair_sems.at[0], pair_sems.at[1], (x, zh * 2 + 1 - c, e))
 
-    for step in range(2, 5):
+    for step in range(COMBINE_AT + 1, 4):
         step2(step)
 
-    arrived(normed.at[1 - c], pair_sems.at[1])
-
-    for n in range(NZH):
-        to = wrap(zh + 2 + n, NZH)
+    def product(k):
+        to = wrap(zh + k, NZH)
 
         def part(q, total):
             left = normed[:, :, pl.ds(pl.multiple_of(q * QUART, QUART), QUART)].reshape(2 * TOK, QUART)
@@ -233,29 +253,40 @@
             return total + jnp.dot(left, right, preferred_element_type=jnp.float32)
 
         total = lax.fori_loop(0, 4, part, jnp.zeros((2 * TOK, NCOL), jnp.float32))
-        result[n] = total.astype(jnp.bfloat16).reshape(2, TOK, NCOL)
+        result[k] = total.astype(jnp.bfloat16).reshape(2, TOK, NCOL)
         remote(
-            result.at[n], out_ref.at[pl.ds(zh * 2, 2)], out_send.at[n], out_recv.at[n],
+            result.at[k], out_ref.at[pl.ds(zh * 2, 2)], out_send.at[k], out_recv.at[k],
             (x_next, to * 2 + c, e),
         )
-    for n in range(NZH):
-        source = wrap(zh - 2 - n, NZH)
-        arrived(out_ref.at[pl.ds(source * 2, 2)], out_recv.at[n])
+
+    step2(4, "y")
+    arrived(normed.at[1 - c], pair_sems.at[1])
+    for k in (0, 1, 3):
+        product(k)
+    step2(4, "z")
+    product(2)
+
+    for k in range(NZH):
+        source = wrap(zh - k, NZH)
+        arrived(out_ref.at[pl.ds(source * 2, 2)], out_recv.at[k])
     for copy in sends:
         copy.wait_send()
 
 
 def body(stream, expert_rows, expert_ids, route_weight, norm_gain, kv_weight):
     rows = jnp.transpose(expert_rows[0], (1, 0, 2)).reshape(CAP * NE, D)
-    vmem = pl.BlockSpec(memory_space=pltpu.VMEM)
     hbm = pl.BlockSpec(memory_space=pl.ANY)
     dma = pltpu.SemaphoreType.DMA
     out = pl.pallas_call(
         kernel,
         out_shape=jax.ShapeDtypeStruct((8, TOK, NCOL), jnp.bfloat16),
-        in_specs=[vmem, vmem, vmem, vmem, hbm, hbm],
+        in_specs=[hbm] * 6,
         out_specs=hbm,
         scratch_shapes=[
+            pltpu.VMEM((CAP * NE, D), jnp.bfloat16),
+            pltpu.VMEM((TOK, D), jnp.bfloat16),
+            pltpu.VMEM((1, TOK), jnp.int32),
+            pltpu.VMEM((1, TOK), jnp.float32),
             pltpu.VMEM((256, PACK), jnp.bfloat16),
             pltpu.VMEM((256, PACK), jnp.bfloat16),
             pltpu.VMEM((NZH, 2, NY, KROWS, NCOL), jnp.bfloat16),
@@ -263,11 +294,11 @@
             pltpu.VMEM((4, TOK, 768), jnp.bfloat16),
             pltpu.VMEM((2, TOK, D), jnp.bfloat16),
             pltpu.VMEM((NZH, 2, TOK, NCOL), jnp.bfloat16),
-            dma((4,)), dma((NE,)), dma((NE,)), dma,
+            dma((4,)), dma((4,)), dma((NE,)), dma((NE,)), dma,
             dma((14,)), dma((14,)), dma((28,)), dma((28,)), dma((2,)), dma((NZH,)), dma((NZH,)),
         ],
         compiler_params=pltpu.CompilerParams(
-            collective_id=0, has_side_effects=True, vmem_limit_bytes=48 * 1024 * 1024
+            collective_id=0, has_side_effects=True, vmem_limit_bytes=63 * 1024 * 1024
         ),
         cost_estimate=pl.CostEstimate(
             flops=2 * 1024 * D * NCOL, bytes_accessed=8 * 1024 * 1024, transcendentals=TOK

time: 159 us -> 140 us (0.88)
  Pallas kernels: 151 us -> 138 us
  local copies, waits for them, and re-layouts: 6.61 us -> 1.87 us
    pallas_call x1, Pallas kernels: 151 us -> 138 us  [body(): pl.pallas_call(kernel, out_shape=jax.ShapeDtypeStruct((8, TOK, NCOL), jnp...]
    unnamed x13 -> x1, local copies, waits for them, and re-layouts: 6.61 us -> 1.87 us
where the time goes in v2:
time: 140 us
  Pallas kernels  138 us (99%)
  local copies, waits for them, and re-layouts  1.87 us (1%)
    pallas_call x1, Pallas kernels, body(): pl.pallas_call(kernel, out_shape=jax.ShapeDtypeStruct((8, TOK, NCOL), jnp...  138 us

profile of v2, /device:TPU:1, one launch (start us, length us, event | category | flops | bytes accessed | tf_op | source)
XLA Modules:
  0.0 140.3 jit_solution(5556035439156465456)
XLA Ops:
  0.0 138.4 %shard_map.64 = bf16[8,128,256]{2,1,0:T(8,128)(2,1)} custom-call(bf16[192,5120]{1,0:T(8,128)(2,1)} %bitcast.12, bf16[128,5120]{1,0:T(8,128)(2,1)} %stream_hbm.1, s32[1,128]{1,0:T(1,128)} %bitcast.14, f32[1,128]{1,0:T(1,128)} %bitcast.15, f32[1,5120]{1,0:T(1,128)} %gain_ref.1, bf16[320,256]{1,0:T(8,128)(2,1)} %bitcast.13), custom_call_target="tpu_custom_call" | custom-call | flops 2684354560 | bytes 8388608 | tf_op jit(solution)/shard_map/pallas_call | solution.py:280
  138.4 1.9 %copy.9 = bf16[8,1,128,256]{3,2,1,0:T(8,128)(2,1)} copy(bf16[8,1,128,256]{3,2,1,0:T(8,128)(2,1)} %bitcast.11) | data formatting | bytes 1048576

commit v3 on v2

--- a/solution.py
+++ b/solution.py
@@ -232,6 +232,9 @@
     total = lax.fori_loop(0, 20, combine, jnp.zeros((TOK, CH), jnp.float32))
     scale = lax.rsqrt(jnp.sum(total, axis=1, keepdims=True) / D + EPS)
 
+    for step in range(COMBINE_AT + 1, 4):
+        step2(step)
+
     def norm(i, _):
         at = pl.ds(pl.multiple_of(i * CH, CH), CH)
         value = normed[c, :, at].astype(jnp.float32) * scale * gain[:, at]
@@ -240,9 +243,6 @@
 
     lax.fori_loop(0, 20, norm, 0)
     remote(normed.at[c], normed.at[c], pair_sems.at[0], pair_sems.at[1], (x, zh * 2 + 1 - c, e))
-
-    for step in range(COMBINE_AT + 1, 4):
-        step2(step)
 
     def product(k):
         to = wrap(zh + k, NZH)

time: 140 us -> 140 us (level)
  no operation moved by 1% of the time
where the time goes in v3:
time: 140 us
  Pallas kernels  138 us (99%)
  local copies, waits for them, and re-layouts  1.87 us (1%)
    pallas_call x1, Pallas kernels, body(): pl.pallas_call(kernel, out_shape=jax.ShapeDtypeStruct((8, TOK, NCOL), jnp...  138 us

profile of v3, /device:TPU:1, one launch (start us, length us, event | category | flops | bytes accessed | tf_op | source)
XLA Modules:
  0.0 140.3 jit_solution(16643162839016742911)
XLA Ops:
  0.0 138.4 %shard_map.64 = bf16[8,128,256]{2,1,0:T(8,128)(2,1)} custom-call(bf16[192,5120]{1,0:T(8,128)(2,1)} %bitcast.12, bf16[128,5120]{1,0:T(8,128)(2,1)} %stream_hbm.1, s32[1,128]{1,0:T(1,128)} %bitcast.14, f32[1,128]{1,0:T(1,128)} %bitcast.15, f32[1,5120]{1,0:T(1,128)} %gain_ref.1, bf16[320,256]{1,0:T(8,128)(2,1)} %bitcast.13), custom_call_target="tpu_custom_call" | custom-call | flops 2684354560 | bytes 8388608 | tf_op jit(solution)/shard_map/pallas_call | solution.py:280
  138.4 1.9 %copy.9 = bf16[8,1,128,256]{3,2,1,0:T(8,128)(2,1)} copy(bf16[8,1,128,256]{3,2,1,0:T(8,128)(2,1)} %bitcast.11) | data formatting | bytes 1048576
